TPU v7x, 32 devices: a whole 2x2x4 slice. The times are simulated.
32 devices in a mesh: dp: 4 (over y, x), expert: 8 (over z, core).
Axes of the slice: x: 2, y: 2, z: 4, core: 2. Of those that a mesh axis runs over, the one named last changes fastest.
Arguments:
- tokens: bfloat16 [4096, 2560], P(('dp', 'expert')), may hold values from -6 to 6
- routes: int32 [4096, 2], P(('dp', 'expert')), may hold values from 0 to 7, all different within a row; in each aligned block of 128 rows (0 to 127, 128 to 255, ...) at most 36 rows name the same one
- route_gates: float32 [4096, 2], P(('dp', 'expert')), may hold values from 0.2 to 1
- w_gate: bfloat16 [8, 2560, 768], P('expert', 'dp'), may hold values from -0.125 to 0.125
- w_up: bfloat16 [8, 2560, 768], P('expert', 'dp'), may hold values from -0.125 to 0.125
- w_down: bfloat16 [8, 768, 2560], P('expert', None, 'dp'), may hold values from -0.21875 to 0.21875
- cotangent: bfloat16 [4096, 2560], P(('dp', 'expert')), may hold values from -6 to 6
Outputs:
- layer_out: bfloat16 [4096, 2560], P(('dp', 'expert'))
- token_grad: bfloat16 [4096, 2560], P(('dp', 'expert'))
- gate_grad: float32 [4096, 2], P(('dp', 'expert'))
Inputs may be any that keep to these rules, and one draw needn't show every extreme that they name: `routes`: among the 128 rows of one device, each expert is named at most 36 times, and in every draw some device names some expert exactly 36 times. The 2 experts of a token differ.
All inputs are finite; a program needn't handle non-finite values.
Results may differ from a plain program's by a relative error of at most 0.0067.
Values may be sent and summed in bfloat16 or wider, within the bound.
A program may use at most 128 MiB of HBM per device.

v0:
```python
import jax
import jax.numpy as jnp
from jax import lax
from jax.sharding import PartitionSpec as P

EXP_DEV = 1


def expert_forward(arriving, gate_full, up_full, down_full):
    gate_pre = jnp.einsum("snd,df->snf", arriving, gate_full, preferred_element_type=jnp.float32)
    up_pre = jnp.einsum("snd,df->snf", arriving, up_full, preferred_element_type=jnp.float32)
    hidden = (gate_pre * jax.nn.sigmoid(gate_pre) * up_pre).astype(jnp.bfloat16)
    expert_out = jnp.einsum(
        "snf,fd->snd", hidden, down_full, preferred_element_type=jnp.float32
    ).astype(jnp.bfloat16)
    return (expert_out, gate_pre, up_pre)


def expert_backward(arriving_grad, gate_pre, up_pre, gate_full, up_full, down_full):
    hidden_grad = jnp.einsum(
        "snd,fd->snf", arriving_grad, down_full, preferred_element_type=jnp.float32
    )
    logistic = jax.nn.sigmoid(gate_pre)
    pre_gate = (hidden_grad * up_pre * logistic * (1.0 + gate_pre * (1.0 - logistic))).astype(
        jnp.bfloat16
    )
    pre_up = (hidden_grad * gate_pre * logistic).astype(jnp.bfloat16)
    input_grad = jnp.einsum("snf,df->snd", pre_gate, gate_full, preferred_element_type=jnp.float32)
    input_grad = input_grad + jnp.einsum(
        "snf,df->snd", pre_up, up_full, preferred_element_type=jnp.float32
    )
    return input_grad.astype(jnp.bfloat16)


def local(tokens, routes, route_gates, w_gate, w_up, w_down, cotangent):
    groups = lax.axis_size("expert")
    tok_rows = tokens.shape[0]
    top_count = routes.shape[1]
    width = tokens.shape[1]
    capacity = 9 * tok_rows * top_count // (8 * groups * EXP_DEV)
    pair_expert = routes.reshape(-1)
    pair_token = jnp.arange(tok_rows * top_count, dtype=jnp.int32) // top_count
    onehot = (pair_expert[:, None] == jnp.arange(groups, dtype=jnp.int32)[None, :]).astype(
        jnp.int32
    )
    slot_rank = jnp.sum((jnp.cumsum(onehot, axis=0) - onehot) * onehot, axis=1)
    slot_place = pair_expert * capacity + slot_rank
    outbox = (
        jnp.zeros((groups * capacity, width), jnp.bfloat16).at[slot_place].set(tokens[pair_token])
    )
    outbox = outbox.reshape(groups, capacity, width)
    pair_gate = route_gates.reshape(-1)
    cot_pairs = cotangent[pair_token].astype(jnp.float32)
    row_grad = (pair_gate[:, None] * cot_pairs).astype(jnp.bfloat16)
    gradbox = jnp.zeros((groups * capacity, width), jnp.bfloat16).at[slot_place].set(row_grad)
    gradbox = gradbox.reshape(groups, capacity, width)
    gate_full, up_full, down_full = (
        lax.all_gather(w_gate[0], "dp", axis=0, tiled=True),
        lax.all_gather(w_up[0], "dp", axis=0, tiled=True),
        lax.all_gather(w_down[0], "dp", axis=1, tiled=True),
    )
    expert_out, gate_pre, up_pre = expert_forward(
        lax.all_to_all(outbox, "expert", split_axis=0, concat_axis=0, tiled=True),
        gate_full,
        up_full,
        down_full,
    )
    returned = lax.all_to_all(expert_out, "expert", split_axis=0, concat_axis=0, tiled=True)
    returned, gate_pre, up_pre = (returned, gate_pre, up_pre)
    arriving_grad = lax.all_to_all(gradbox, "expert", split_axis=0, concat_axis=0, tiled=True)
    input_grad = expert_backward(arriving_grad, gate_pre, up_pre, gate_full, up_full, down_full)
    back_grad = lax.all_to_all(input_grad, "expert", split_axis=0, concat_axis=0, tiled=True)
    pair_out = returned.reshape(groups * capacity, width)[slot_place].astype(jnp.float32)
    layer_out = jnp.sum(
        (pair_gate[:, None] * pair_out).reshape(tok_rows, top_count, width), axis=1
    ).astype(jnp.bfloat16)
    gate_grad = jnp.sum(cot_pairs * pair_out, axis=1).reshape(tok_rows, top_count)
    pair_grad = back_grad.reshape(groups * capacity, width)[slot_place].astype(jnp.float32)
    token_grad = jnp.sum(pair_grad.reshape(tok_rows, top_count, width), axis=1).astype(jnp.bfloat16)
    return (layer_out, token_grad, gate_grad)


def solution(mesh):
    in_specs = (
        P(("dp", "expert"), None),
        P(("dp", "expert"), None),
        P(("dp", "expert"), None),
        P("expert", "dp", None),
        P("expert", "dp", None),
        P("expert", None, "dp"),
        P(("dp", "expert"), None),
    )
    out_specs = (P(("dp", "expert"), None), P(("dp", "expert"), None), P(("dp", "expert"), None))
    return jax.shard_map(local, mesh=mesh, in_specs=in_specs, out_specs=out_specs, check_vma=False)
```

profile of v0, /device:TPU:25, one launch (start us, length us, event | category | flops | bytes accessed | tf_op | source)
XLA Modules:
  0.0 282.3 jit_solution(3171517548182173325)
XLA Ops:
  11.1 6.9 %scatter_custom_fusion = bf16[288,2560]{1,0:T(8,128)(2,1)S(1)} fusion(s32[256]{0:T(256)S(1)} %bitcast.34, bf16[128,2560]{1,0:T(8,128)(2,1)S(1)} %copy-done, s32[1024]{0:T(1024)S(1)} %pad_clamp_fusion.1, bf16[]{:T(256)} %constant.26.clone.1), kind=kCustom, calls=%fused_computation.25 | custom fusion | bytes 1474562 | tf_op jit(solution)/shard_map/scatter | solution.py:49
  19.3 5.5 %all-to-all-start = ((bf16[8,36,2560]{2,1,0:T(8,128)(2,1)}), bf16[8,36,2560]{2,1,0:T(8,128)(2,1)}, u32[]{:S(2)}, u32[]{:S(2)}) async-start(bf16[8,36,2560]{2,1,0:T(8,128)(2,1)} %reshape.123), calls=%async_computation | async-start | bytes 3276800 | tf_op jit(solution)/shard_map/all_to_all | solution.py:63
  26.6 3.1 %scatter_custom_fusion.1 = bf16[288,2560]{1,0:T(8,128)(2,1)S(1)} fusion(s32[256]{0:T(256)S(1)} %bitcast.35, bf16[256,2560]{1,0:T(8,128)(2,1)S(1)} %gather_fusion.1, f32[256]{0:T(256)S(1)} %mul.73, bf16[]{:T(256)} %constant.26.clone.1), kind=kCustom, calls=%fused_computation.24 | custom fusion | flops 1966080 | bytes 2786306 | tf_op jit(solution)/shard_map/scatter | solution.py:55
  31.2 30.4 %all-to-all-done = bf16[8,36,2560]{2,1,0:T(8,128)(2,1)} async-done(((bf16[8,36,2560]{2,1,0:T(8,128)(2,1)}), bf16[8,36,2560]{2,1,0:T(8,128)(2,1)}, u32[]{:S(2)}, u32[]{:S(2)}) %all-to-all-start) | async-done | bytes 1474592 | tf_op jit(solution)/shard_map/all_to_all | solution.py:63
  61.6 6.9 %all-to-all-start.2 = ((bf16[8,36,2560]{2,1,0:T(8,128)(2,1)}), bf16[8,36,2560]{2,1,0:T(8,128)(2,1)}, u32[]{:S(2)}, u32[]{:S(2)}) async-start(bf16[8,36,2560]{2,1,0:T(8,128)(2,1)} %reshape.125), calls=%async_computation.2 | async-start | bytes 3276800 | tf_op jit(solution)/shard_map/all_to_all | solution.py:70
  68.4 4.3 %fusion.9 = f32[8,36,768]{2,1,0:T(8,128)S(1)} fusion(bf16[8,36,2560]{2,1,0:T(8,128)(2,1)} %all-to-all-done, bf16[1,2560,768]{2,1,0:T(8,128)(2,1)} %all-gather.7.cloned.1.call-done), kind=kOutput, calls=%fused_computation.17 | convolution fusion | flops 1132462080 | bytes 6291456 | tf_op jit(solution)/shard_map/snd,df->snf/dot_general | solution.py:10
  72.7 41.1 %all-gather.9.cloned.1.call-done = bf16[1,2560,768]{2,1,0:T(8,128)(2,1)} async-done(((bf16[1,640,768]{2,1,0:T(8,128)(2,1)}), bf16[1,2560,768]{2,1,0:T(8,128)(2,1)}) %all-gather.9.cloned.1.call-update) | async-done | bytes 3932176 | tf_op jit(solution)/shard_map/all_gather | solution.py:59
  113.8 5.0 %fusion.5 = f32[8,36,768]{2,1,0:T(8,128)} fusion(bf16[8,36,2560]{2,1,0:T(8,128)(2,1)} %all-to-all-done, bf16[1,2560,768]{2,1,0:T(8,128)(2,1)} %all-gather.9.cloned.1.call-done), kind=kOutput, calls=%fused_computation.13 | convolution fusion | flops 1132462080 | bytes 6291456 | tf_op jit(solution)/shard_map/snd,df->snf/dot_general | solution.py:11
  118.8 47.4 %all-gather.11.cloned.1.call-done = bf16[1,768,2560]{2,1,0:T(8,128)(2,1)} async-done(((bf16[1,768,640]{2,1,0:T(8,128)(2,1)}), bf16[1,768,2560]{2,1,0:T(8,128)(2,1)}) %all-gather.11.cloned.1.call-update) | async-done | bytes 3932176 | tf_op jit(solution)/shard_map/all_gather | solution.py:60
  166.2 5.1 %convolution_convert_fusion = bf16[8,36,2560]{2,1,0:T(8,128)(2,1)} fusion(bf16[1,768,2560]{2,1,0:T(8,128)(2,1)} %all-gather.11.cloned.1.call-done, f32[8,36,768]{2,1,0:T(8,128)} %fusion.5, f32[8,36,768]{2,1,0:T(8,128)S(1)} %fusion.9), kind=kOutput, calls=%fused_computation.8 | convolution fusion | flops 1134526464 | bytes 7176192 | tf_op jit(solution)/shard_map/snf,fd->snd/dot_general | solution.py:13
  171.3 5.4 %all-to-all-start.1 = ((bf16[8,36,2560]{2,1,0:T(8,128)(2,1)}), bf16[8,36,2560]{2,1,0:T(8,128)(2,1)}, u32[]{:S(2)}, u32[]{:S(2)}) async-start(bf16[8,36,2560]{2,1,0:T(8,128)(2,1)} %convolution_convert_fusion), calls=%async_computation.1 | async-start | bytes 3276800 | tf_op jit(solution)/shard_map/all_to_all | solution.py:68
  176.7 4.2 %fusion.1 = f32[8,36,768]{2,1,0:T(8,128)S(1)} fusion(bf16[8,36,2560]{2,1,0:T(8,128)(2,1)} %all-to-all-done.2, bf16[1,768,2560]{2,1,0:T(8,128)(2,1)} %all-gather.11.cloned.1.call-done), kind=kOutput, calls=%fused_computation.9 | convolution fusion | flops 1132462080 | bytes 6291456 | tf_op jit(solution)/shard_map/snd,fd->snf/dot_general | solution.py:20
  181.0 1.7 fusion.7
  183.1 2.7 fusion
  185.8 27.6 %all-to-all-done.1 = bf16[8,36,2560]{2,1,0:T(8,128)(2,1)} async-done(((bf16[8,36,2560]{2,1,0:T(8,128)(2,1)}), bf16[8,36,2560]{2,1,0:T(8,128)(2,1)}, u32[]{:S(2)}, u32[]{:S(2)}) %all-to-all-start.1) | async-done | bytes 1474592 | tf_op jit(solution)/shard_map/all_to_all | solution.py:68
  213.4 6.9 %all-to-all-start.3 = ((bf16[8,36,2560]{2,1,0:T(8,128)(2,1)}), bf16[8,36,2560]{2,1,0:T(8,128)(2,1)}, u32[]{:S(2)}, u32[]{:S(2)}) async-start(bf16[8,36,2560]{2,1,0:T(8,128)(2,1)} %fusion), calls=%async_computation.3 | async-start | bytes 3276800 | tf_op jit(solution)/shard_map/all_to_all | solution.py:72
  220.3 1.6 reshape.124
  221.9 2.5 gather_fusion
  224.4 4.2 %reshape.128 = f32[128,2,2560]{2,1,0:T(2,128)} reshape(bf16[256,2560]{1,0:T(8,128)(2,1)} %gather_fusion) | data formatting | bytes 3932160 | tf_op jit(solution)/shard_map/convert_element_type | solution.py:73
  229.1 27.9 %all-to-all-done.3 = bf16[8,36,2560]{2,1,0:T(8,128)(2,1)} async-done(((bf16[8,36,2560]{2,1,0:T(8,128)(2,1)}), bf16[8,36,2560]{2,1,0:T(8,128)(2,1)}, u32[]{:S(2)}, u32[]{:S(2)}) %all-to-all-start.3) | async-done | bytes 1474592 | tf_op jit(solution)/shard_map/all_to_all | solution.py:72
  258.5 2.5 gather_fusion.2
  261.0 4.1 %gather.18 = bf16[128,2,2560]{2,1,0:T(2,128)(2,1)} reshape(bf16[256,2560]{1,0:T(8,128)(2,1)} %gather_fusion.2) | data formatting | bytes 2621440 | tf_op jit(solution)/shard_map/gather | solution.py:78
  265.1 5.3 %reduce_sum.44 = bf16[128,2560]{1,0:T(8,128)(2,1)} reduce(bf16[128,2,2560]{2,1,0:T(2,128)(2,1)} %gather.18, bf16[]{:T(256)} %constant.26.clone.1), dimensions={1}, to_apply=%region_6.7 | reduce | flops 327680 | bytes 1966082 | tf_op jit(solution)/shard_map/reduce_sum | solution.py:79
  271.2 4.5 %multiply_reduce_fusion = bf16[128,2560]{1,0:T(8,128)(2,1)} fusion(f32[128,2,2560]{2,1,0:T(2,128)S(1)} %copy-done.3, f32[128,2]{1,0:T(8,128)S(1)} %copy.11), kind=kLoop, calls=%fused_computation.23 | loop fusion | flops 983040 | bytes 3277824 | tf_op jit(solution)/shard_map/reduce_sum | solution.py:74
  (51 shorter events, 11.5 us)
Async XLA Ops:
  7.2 3.9 %copy-start = (bf16[128,2560]{1,0:T(8,128)(2,1)S(1)}, bf16[128,2560]{1,0:T(8,128)(2,1)}, u32[]{:S(2)}) copy-start(bf16[128,2560]{1,0:T(8,128)(2,1)} %param.7) | copy-start | bytes 1966084
  7.2 2.2 copy-start.4
  7.2 61.2 %all-gather.7.cloned.1.call-start = ((), (), s32[]{:S(2)}) async-start(), calls=%async_computation.4 | async-start | bytes 4915200 | tf_op jit(solution)/shard_map/all_gather | solution.py:58
  7.9 105.9 %all-gather.9.cloned.1.call-start = ((), (), s32[]{:S(2)}) async-start(), calls=%async_computation.5 | async-start | bytes 4915200 | tf_op jit(solution)/shard_map/all_gather | solution.py:59
  8.7 157.5 %all-gather.11.cloned.1.call-start = ((), (), s32[]{:S(2)}) async-start(), calls=%async_computation.6 | async-start | bytes 4915200 | tf_op jit(solution)/shard_map/all_gather | solution.py:60
  19.3 5.6 %copy-start.5 = (f32[128,2]{0,1:T(2,128)S(1)}, f32[128,2]{0,1:T(2,128)}, u32[]{:S(2)}) copy-start(f32[128,2]{0,1:T(2,128)} %param.9) | copy-start | bytes 3076
  19.3 5.8 %copy-start.1 = (bf16[128,2560]{1,0:T(8,128)(2,1)S(1)}, bf16[128,2560]{1,0:T(8,128)(2,1)}, u32[]{:S(2)}) copy-start(bf16[128,2560]{1,0:T(8,128)(2,1)} %param.13) | copy-start | bytes 1966084
  19.3 42.2 %all-to-all-start = ((bf16[8,36,2560]{2,1,0:T(8,128)(2,1)}), bf16[8,36,2560]{2,1,0:T(8,128)(2,1)}, u32[]{:S(2)}, u32[]{:S(2)}) async-start(bf16[8,36,2560]{2,1,0:T(8,128)(2,1)} %reshape.123), calls=%async_computation | async-start | bytes 3276800 | tf_op jit(solution)/shard_map/all_to_all | solution.py:63
  61.6 109.8 %all-to-all-start.2 = ((bf16[8,36,2560]{2,1,0:T(8,128)(2,1)}), bf16[8,36,2560]{2,1,0:T(8,128)(2,1)}, u32[]{:S(2)}, u32[]{:S(2)}) async-start(bf16[8,36,2560]{2,1,0:T(8,128)(2,1)} %reshape.125), calls=%async_computation.2 | async-start | bytes 3276800 | tf_op jit(solution)/shard_map/all_to_all | solution.py:70
  171.3 42.1 %all-to-all-start.1 = ((bf16[8,36,2560]{2,1,0:T(8,128)(2,1)}), bf16[8,36,2560]{2,1,0:T(8,128)(2,1)}, u32[]{:S(2)}, u32[]{:S(2)}) async-start(bf16[8,36,2560]{2,1,0:T(8,128)(2,1)} %convolution_convert_fusion), calls=%async_computation.1 | async-start | bytes 3276800 | tf_op jit(solution)/shard_map/all_to_all | solution.py:68
  176.7 4.2 %copy-start.6 = (bf16[1,2560,768]{2,1,0:T(8,128)(2,1)S(1)}, bf16[1,2560,768]{2,1,0:T(8,128)(2,1)}, u32[]{:S(2)}) copy-start(bf16[1,2560,768]{2,1,0:T(8,128)(2,1)} %all-gather.7.cloned.1.call-done) | copy-start | bytes 11796484
  176.7 4.2 %copy-start.8 = (f32[8,36,768]{2,1,0:T(8,128)S(1)}, f32[8,36,768]{2,1,0:T(8,128)}, u32[]{:S(2)}) copy-start(f32[8,36,768]{2,1,0:T(8,128)} %fusion.5) | copy-start | bytes 2654212
  181.0 2.1 copy-start.7
  213.4 43.5 %all-to-all-start.3 = ((bf16[8,36,2560]{2,1,0:T(8,128)(2,1)}), bf16[8,36,2560]{2,1,0:T(8,128)(2,1)}, u32[]{:S(2)}, u32[]{:S(2)}) async-start(bf16[8,36,2560]{2,1,0:T(8,128)(2,1)} %fusion), calls=%async_computation.3 | async-start | bytes 3276800 | tf_op jit(solution)/shard_map/all_to_all | solution.py:72
  224.4 4.2 %copy-start.2 = (bf16[256,2560]{1,0:T(8,128)(2,1)S(1)}, bf16[256,2560]{1,0:T(8,128)(2,1)}, u32[]{:S(2)}) copy-start(bf16[256,2560]{1,0:T(8,128)(2,1)} %gather_fusion) | copy-start | bytes 3932164
  261.0 10.2 %copy-start.3 = (f32[128,2,2560]{2,1,0:T(2,128)S(1)}, f32[128,2,2560]{2,1,0:T(2,128)}, u32[]{:S(2)}) copy-start(f32[128,2,2560]{2,1,0:T(2,128)} %reshape.128) | copy-start | bytes 7864324
Sparse Core Ops, SparseCore 0:
  9.9 51.4 all-gather.6
  63.3 50.5 all-gather.8
  115.7 50.5 all-gather.10
where the time goes:
time: 286 us; the launch traced here: 282 us
  waiting for transfers between devices  176 us (62%)
  local copies, waits for them, and re-layouts  29.9 us (10%)
  starting transfers between devices  24.8 us (9%)
  matrix products  23 us (8%)
  other arithmetic  14.1 us (5%)
  between operations  13.9 us (5%)
    all_gather x1, waiting for transfers between devices, local(): lax.all_gather(w_down[0], 'dp', axis=1, tiled=True)  47.4 us
    all_gather x1, waiting for transfers between devices, local(): lax.all_gather(w_up[0], 'dp', axis=0, tiled=True)  41.1 us
    all_to_all x1, waiting for transfers between devices, local(): lax.all_to_all(outbox, 'expert', split_axis=0, concat_axis=0, tiled=True)  30.4 us
    all_to_all x1, waiting for transfers between devices, local(): lax.all_to_all(input_grad, 'expert', split_axis=0, concat_axis=0, tiled=T...  27.9 us
    all_to_all x1, waiting for transfers between devices, local(): lax.all_to_all(expert_out, 'expert', split_axis=0, concat_axis=0, tiled=T...  27.6 us
    scatter x1, local copies, waits for them, and re-layouts, local(): jnp.zeros((groups * capacity, width), jnp.bfloat16).at[slot_place]  6.87 us
    all_to_all x1, starting transfers between devices, local(): lax.all_to_all(gradbox, 'expert', split_axis=0, concat_axis=0, tiled=True)  6.86 us
    all_to_all x1, starting transfers between devices, local(): lax.all_to_all(input_grad, 'expert', split_axis=0, concat_axis=0, tiled=T...  6.85 us
  transfers between devices with their start and end apart: 7, of which 5 were waited for; matrix products, arithmetic and copies ran while one was open for 17% of the time, Pallas kernels for 0%

commit v1 on v0

v1 whole, which is shorter than its diff:
```python
import functools

import jax
import jax.numpy as jnp
from jax import lax
from jax.experimental import pallas as pl
from jax.experimental.pallas import tpu as pltpu
from jax.sharding import PartitionSpec as P

BF = jnp.bfloat16
F32 = jnp.float32
NN = (((1,), (0,)), ((), ()))
NT = (((1,), (1,)), ((), ()))


def dot(a, b, dims=NN):
    return lax.dot_general(a, b, dims, preferred_element_type=F32)


def moe_kernel(
    E,
    MAIN,
    REM,
    tok_ref, cot_ref, routes_ref, gates_ref, routes_t_ref, gates_t_ref,
    wg_ref, wu_ref, wd_ref,
    lo_ref, tg_ref, gg_ref,
    wg, wu, wd,
    tok_out, grd_out, tok_in, grd_in,
    res_out, res_in, ig_out, ig_in,
    xs, gs, s_main, s_ext, p_main, p_ext,
    gate_pre, up_pre, hid_grad, hidden, pre_gate, pre_up,
    loc_sem, ws_sem, wr_sem,
    ts_sem, tr_sem, gs_sem, gr_sem,
    os_sem, or_sem, is_sem, ir_sem,
):
    T = tok_ref.shape[0]
    NB = 4
    CB = tok_ref.shape[1] // NB
    FOLD = 16 // REM
    XROW = NB * MAIN
    EXT = E * 16
    UNF = E * REM
    ROWS = E * MAIN
    dp = lax.axis_index("dp")
    me = lax.axis_index("expert")
    xp = dp + 1 - 2 * lax.rem(dp, 2)
    yp = lax.rem(dp + 2, 4)
    dg = 3 - dp

    barrier = pltpu.get_barrier_semaphore()
    for o in range(1, 4):
        pl.semaphore_signal(barrier, inc=1, device_id={"dp": lax.rem(dp + o, 4)}, device_id_type=pl.DeviceIdType.MESH)
    for o in range(1, E):
        pl.semaphore_signal(barrier, inc=1, device_id={"expert": lax.rem(me + o, E)}, device_id_type=pl.DeviceIdType.MESH)
    pl.semaphore_wait(barrier, 3 + E - 1)

    mats = ((wg_ref, wg), (wu_ref, wu), (wd_ref, wd))

    def remote(src, dst, s, r, axis, to):
        return pltpu.make_async_remote_copy(
            src_ref=src, dst_ref=dst, send_sem=s, recv_sem=r, device_id={axis: to}, device_id_type=pl.DeviceIdType.MESH
        )

    def own(m, j):
        src, buf = mats[m]
        return remote(src.at[0], buf.at[dp], ws_sem.at[m, j], wr_sem.at[m, j], "dp", (xp, yp)[j])

    def own_arrived(m, j):
        src, buf = mats[m]
        b = (xp, yp)[j]
        return remote(src.at[0], buf.at[b], ws_sem.at[m, j], wr_sem.at[m, j], "dp", b)

    def relay(m, j):
        buf = mats[m][1]
        half = buf.shape[1] // 2
        b, to = ((xp, yp), (yp, xp))[j]
        part = buf.at[b, pl.ds(j * half, half)]
        return remote(part, part, ws_sem.at[m, 2 + j], wr_sem.at[m, 2 + j], "dp", to)

    def relay_arrived(m, j):
        buf = mats[m][1]
        half = buf.shape[1] // 2
        part = buf.at[dg, pl.ds(j * half, half)]
        return remote(part, part, ws_sem.at[m, 2 + j], wr_sem.at[m, 2 + j], "dp", (yp, xp)[j])

    for m in range(2):
        for j in range(2):
            own(m, j).start()
    locs = [pltpu.make_async_copy(src.at[0], buf.at[dp], loc_sem.at[m]) for m, (src, buf) in enumerate(mats)]
    for c in locs:
        c.start()

    r_t = routes_t_ref[...]
    g_t = gates_t_ref[...]
    row_e = lax.broadcasted_iota(jnp.int32, (E, T), 0)
    hit0 = r_t[0:1, :] == row_e
    hit1 = r_t[1:2, :] == row_e
    hit = jnp.logical_or(hit0, hit1)
    before = lax.broadcasted_iota(jnp.int32, (T, T), 0) < lax.broadcasted_iota(jnp.int32, (T, T), 1)
    rank_t = dot(jnp.where(hit, 1.0, 0.0).astype(BF), jnp.where(before, 1.0, 0.0).astype(BF)).astype(jnp.int32)
    rank_t = jnp.where(hit, rank_t, -1)
    gate_t = jnp.where(hit0, g_t[0:1, :], 0.0) + jnp.where(hit1, g_t[1:2, :], 0.0)
    gsel, gsel_x = [], []
    row_m = lax.broadcasted_iota(jnp.int32, (MAIN, T), 0)
    row_x = lax.broadcasted_iota(jnp.int32, (16, T), 0)
    for e in range(E):
        rank_e = rank_t[e : e + 1, :]
        gate_e = gate_t[e : e + 1, :]
        sel = row_m == rank_e
        s_main[pl.ds(e * MAIN, MAIN), :] = jnp.where(sel, 1.0, 0.0).astype(BF)
        gsel.append(jnp.sum(jnp.where(sel, gate_e, 0.0), axis=1, keepdims=True))
        total = jnp.zeros((16, 1), F32)
        for q in range(FOLD):
            sel = jnp.logical_and(
                row_x - q * REM + MAIN == rank_e,
                jnp.logical_and(rank_e >= MAIN, jnp.logical_and(row_x >= q * REM, row_x < q * REM + REM)),
            )
            s_ext[q, pl.ds(e * 16, 16), :] = jnp.where(sel, 1.0, 0.0).astype(BF)
            total = total + jnp.sum(jnp.where(sel, gate_e, 0.0), axis=1, keepdims=True)
        gsel_x.append(total)
    gsel = jnp.concatenate(gsel, axis=0)
    gsel_x = jnp.concatenate(gsel_x, axis=0)

    def pack(src_ref, box, scale, scale_x):
        ext = jnp.zeros((EXT, CB), F32)
        for b in range(NB):
            block = src_ref[:, b * CB : (b + 1) * CB]
            rows = dot(s_main[...], block)
            if scale is not None:
                rows = rows * scale
            box[:, pl.ds(b * MAIN, MAIN), :] = rows.astype(BF).reshape(E, MAIN, CB)
            ext = ext + dot(s_ext[b], block)
        if scale is not None:
            ext = ext * scale_x
        box[:, pl.ds(XROW, 16), :] = ext.astype(BF).reshape(E, 16, CB)

    def exchange(src, dst, s, r, o):
        to = lax.rem(me + o, E)
        return remote(src.at[to], dst.at[me], s.at[o], r.at[o], "expert", to)

    def arrived(src, dst, s, r, o):
        frm = lax.rem(me + E - o, E)
        return remote(src.at[frm], dst.at[frm], s.at[o], r.at[o], "expert", frm)

    pack(tok_ref, tok_out, None, None)
    for o in range(1, E):
        exchange(tok_out, tok_in, ts_sem, tr_sem, o).start()
    tok_in[pl.ds(me, 1)] = tok_out[pl.ds(me, 1)]
    pack(cot_ref, grd_out, gsel, gsel_x)
    for o in range(1, E):
        exchange(grd_out, grd_in, gs_sem, gr_sem, o).start()
    grd_in[pl.ds(me, 1)] = grd_out[pl.ds(me, 1)]

    lane_t = lax.broadcasted_iota(jnp.int32, (T, 128), 1)
    e_of = [routes_ref[:, k : k + 1] for k in range(2)]
    named = jnp.logical_or(e_of[0] == lane_t, e_of[1] == lane_t)
    after = lax.broadcasted_iota(jnp.int32, (T, T), 0) > lax.broadcasted_iota(jnp.int32, (T, T), 1)
    rank = dot(jnp.where(after, 1.0, 0.0).astype(BF), jnp.where(named, 1.0, 0.0).astype(BF))
    lane_m = lax.broadcasted_iota(jnp.int32, (T, ROWS), 1)
    lane_x = lax.broadcasted_iota(jnp.int32, (T, EXT), 1)
    for k in range(2):
        rk = jnp.sum(jnp.where(lane_t == e_of[k], rank, 0.0), axis=1, keepdims=True).astype(jnp.int32)
        place = jnp.where(rk < MAIN, e_of[k] * MAIN + rk, -1)
        p_main[k] = jnp.where(lane_m == place, 1.0, 0.0).astype(BF)
        for q in range(FOLD):
            place = jnp.where(rk >= MAIN, e_of[k] * 16 + q * REM + rk - MAIN, -1)
            p_ext[k, q] = jnp.where(lane_x == place, 1.0, 0.0).astype(BF)

    for m in range(2):
        for j in range(2):
            own_arrived(m, j).wait_recv()
            relay(m, j).start()

    u_row = lax.broadcasted_iota(jnp.int32, (UNF, EXT), 0)
    u_col = lax.broadcasted_iota(jnp.int32, (UNF, EXT), 1)
    f_row = lax.broadcasted_iota(jnp.int32, (EXT, UNF), 0)
    f_col = lax.broadcasted_iota(jnp.int32, (EXT, UNF), 1)

    def unfold(q):
        same = (u_row // REM) * 16 + lax.rem(u_row, REM) + q * REM == u_col
        return jnp.where(same, 1.0, 0.0).astype(BF)

    def fold(q):
        same = (f_col // REM) * 16 + lax.rem(f_col, REM) + q * REM == f_row
        return jnp.where(same, 1.0, 0.0).astype(BF)

    def unpack(box, dst):
        ext = box[:, pl.ds(XROW, 16), :].reshape(EXT, CB)
        for b in range(NB):
            dst[b, pl.ds(0, ROWS), :] = box[:, pl.ds(b * MAIN, MAIN), :].reshape(ROWS, CB)
            dst[b, pl.ds(ROWS, UNF), :] = dot(unfold(b), ext).astype(BF)

    for o in range(1, E):
        arrived(tok_out, tok_in, ts_sem, tr_sem, o).wait_recv()
    unpack(tok_in, xs)
    locs[0].wait()
    locs[1].wait()
    for j in range(2):
        relay_arrived(0, j).wait_recv()
    own(2, 0).start()
    own(2, 1).start()

    def add_gate(b, c):
        gate_pre[...] += dot(xs[b], wg[b])
        return c

    def add_up(b, c):
        up_pre[...] += dot(xs[b], wu[b])
        return c

    gate_pre[...] = jnp.zeros_like(gate_pre)
    up_pre[...] = jnp.zeros_like(up_pre)
    lax.fori_loop(0, NB, add_gate, 0)
    for j in range(2):
        relay_arrived(1, j).wait_recv()
    lax.fori_loop(0, NB, add_up, 0)
    gp = gate_pre[...]
    hidden[...] = (gp * jax.nn.sigmoid(gp) * up_pre[...]).astype(BF)

    def back(src, dst, s, r, i, o, start, size, to, at):
        part = pl.ds(start, size)
        return remote(src.at[to, part], dst.at[at, part], s.at[i, o], r.at[i, o], "expert", to)

    ext_sum = [jnp.zeros((EXT, CB), F32)]

    def result(i, b):
        out = dot(hidden[...], wd[b]).astype(BF)
        start = pl.multiple_of(b * MAIN, MAIN)
        res_out[:, pl.ds(start, MAIN), :] = out[:ROWS].reshape(E, MAIN, CB)
        for o in range(1, E):
            back(res_out, res_in, os_sem, or_sem, i, o, start, MAIN, lax.rem(me + o, E), me).start()
        ext_sum[0] = ext_sum[0] + dot(fold(b), out[ROWS:])

    locs[2].wait()
    result(0, dp)
    for o in range(1, E):
        arrived(grd_out, grd_in, gs_sem, gr_sem, o).wait_recv()
    unpack(grd_in, gs)
    for j in range(2):
        own_arrived(2, j).wait_recv()
        relay(2, j).start()
    result(1, xp)
    result(2, yp)

    def add_grad(b):
        hid_grad[...] += dot(gs[b], wd[b], NT)

    hid_grad[...] = jnp.zeros_like(hid_grad)
    for b in (dp, xp, yp):
        add_grad(b)
    for j in range(2):
        relay_arrived(2, j).wait_recv()
    result(3, dg)
    res_out[:, pl.ds(XROW, 16), :] = ext_sum[0].astype(BF).reshape(E, 16, CB)
    for o in range(1, E):
        back(res_out, res_in, os_sem, or_sem, 4, o, XROW, 16, lax.rem(me + o, E), me).start()
    res_in[pl.ds(me, 1)] = res_out[pl.ds(me, 1)]
    add_grad(dg)

    gp = gate_pre[...]
    up = up_pre[...]
    hg = hid_grad[...]
    sg = jax.nn.sigmoid(gp)
    pre_gate[...] = (hg * up * sg * (1.0 + gp * (1.0 - sg))).astype(BF)
    pre_up[...] = (hg * gp * sg).astype(BF)
    ext = jnp.zeros((EXT, CB), F32)
    for b in range(NB):
        grad = (dot(pre_gate[...], wg[b], NT) + dot(pre_up[...], wu[b], NT)).astype(BF)
        ig_out[:, pl.ds(b * MAIN, MAIN), :] = grad[:ROWS].reshape(E, MAIN, CB)
        ext = ext + dot(fold(b), grad[ROWS:])
        size = MAIN
        if b == NB - 1:
            ig_out[:, pl.ds(XROW, 16), :] = ext.astype(BF).reshape(E, 16, CB)
            size = MAIN + 16
        for o in range(1, E):
            back(ig_out, ig_in, is_sem, ir_sem, b, o, b * MAIN, size, lax.rem(me + o, E), me).start()
    ig_in[pl.ds(me, 1)] = ig_out[pl.ds(me, 1)]

    for i, b in enumerate((dp, xp, yp, dg)):
        for o in range(1, E):
            frm = lax.rem(me + E - o, E)
            back(res_out, res_in, os_sem, or_sem, i, o, pl.multiple_of(b * MAIN, MAIN), MAIN, frm, frm).wait_recv()
    for o in range(1, E):
        frm = lax.rem(me + E - o, E)
        back(res_out, res_in, os_sem, or_sem, 4, o, XROW, 16, frm, frm).wait_recv()

    def pairs(box, b, ext):
        rows = box[:, pl.ds(b * MAIN, MAIN), :].reshape(ROWS, CB)
        return [dot(p_main[k], rows) + dot(p_ext[k, b], ext) for k in range(2)]

    ext = res_in[:, pl.ds(XROW, 16), :].reshape(EXT, CB)
    dots = [jnp.zeros((T, 1), F32) for _ in range(2)]
    for b in range(NB):
        cols = slice(b * CB, (b + 1) * CB)
        two = pairs(res_in, b, ext)
        cot = cot_ref[:, cols].astype(F32)
        lo_ref[:, cols] = (gates_ref[:, 0:1] * two[0] + gates_ref[:, 1:2] * two[1]).astype(BF)
        dots = [dots[k] + jnp.sum(cot * two[k], axis=1, keepdims=True) for k in range(2)]
    gg_ref[...] = jnp.concatenate(dots, axis=1)

    for b in range(NB):
        size = MAIN + 16 if b == NB - 1 else MAIN
        for o in range(1, E):
            frm = lax.rem(me + E - o, E)
            back(ig_out, ig_in, is_sem, ir_sem, b, o, b * MAIN, size, frm, frm).wait_recv()
    ext = ig_in[:, pl.ds(XROW, 16), :].reshape(EXT, CB)
    for b in range(NB):
        two = pairs(ig_in, b, ext)
        tg_ref[:, b * CB : (b + 1) * CB] = (two[0] + two[1]).astype(BF)

    for m in range(3):
        for j in range(2):
            own(m, j).wait_send()
            relay(m, j).wait_send()
    for o in range(1, E):
        exchange(tok_out, tok_in, ts_sem, tr_sem, o).wait_send()
        exchange(grd_out, grd_in, gs_sem, gr_sem, o).wait_send()
        to = lax.rem(me + o, E)
        for i, b in enumerate((dp, xp, yp, dg)):
            back(res_out, res_in, os_sem, or_sem, i, o, pl.multiple_of(b * MAIN, MAIN), MAIN, to, me).wait_send()
        back(res_out, res_in, os_sem, or_sem, 4, o, XROW, 16, to, me).wait_send()
        for b in range(NB):
            size = MAIN + 16 if b == NB - 1 else MAIN
            back(ig_out, ig_in, is_sem, ir_sem, b, o, b * MAIN, size, to, me).wait_send()


def fused(MAIN, REM, tokens, routes, route_gates, w_gate, w_up, w_down, cotangent):
    E = lax.axis_size("expert")
    T, D = tokens.shape
    CB = D // 4
    FF = w_gate.shape[2]
    BOX = 4 * MAIN + 16
    R = E * (MAIN + REM)
    box = pltpu.VMEM((E, BOX, CB), BF)
    vm = pl.BlockSpec(memory_space=pltpu.VMEM)
    hb = pl.BlockSpec(memory_space=pl.ANY)
    dma = pltpu.SemaphoreType.DMA
    return pl.pallas_call(
        functools.partial(moe_kernel, E, MAIN, REM),
        out_shape=(
            jax.ShapeDtypeStruct((T, D), BF),
            jax.ShapeDtypeStruct((T, D), BF),
            jax.ShapeDtypeStruct((T, 2), F32),
        ),
        in_specs=[vm] * 6 + [hb] * 3,
        out_specs=(vm, vm, vm),
        scratch_shapes=[
            pltpu.VMEM((4, CB, FF), BF), pltpu.VMEM((4, CB, FF), BF), pltpu.VMEM((4, FF, CB), BF),
            box, box, box, box,
            box, box, box, box,
            pltpu.VMEM((4, R, CB), BF), pltpu.VMEM((4, R, CB), BF),
            pltpu.VMEM((E * MAIN, T), BF), pltpu.VMEM((16 // REM, E * 16, T), BF),
            pltpu.VMEM((2, T, E * MAIN), BF), pltpu.VMEM((2, 16 // REM, T, E * 16), BF),
            pltpu.VMEM((R, FF), F32), pltpu.VMEM((R, FF), F32), pltpu.VMEM((R, FF), F32),
            pltpu.VMEM((R, FF), BF), pltpu.VMEM((R, FF), BF), pltpu.VMEM((R, FF), BF),
            dma((3,)), dma((3, 4)), dma((3, 4)),
            dma((E,)), dma((E,)), dma((E,)), dma((E,)),
            dma((5, E)), dma((5, E)), dma((4, E)), dma((4, E)),
        ],
        compiler_params=pltpu.CompilerParams(
            collective_id=0, has_side_effects=True, vmem_limit_bytes=56 * 1024 * 1024
        ),
    )(tokens, cotangent, routes, route_gates, routes.T, route_gates.T, w_gate, w_up, w_down)


def gather(x, axis):
    n = lax.axis_size("dp")
    me = lax.axis_index("dp")
    width = x.shape[axis]
    shape = list(x.shape)
    shape[axis] = n * width
    full = lax.dynamic_update_slice_in_dim(jnp.zeros(shape, x.dtype), x, me * width, axis)
    part = x
    for step in range(1, n):
        part = lax.ppermute(part, "dp", [(i, (i + 1) % n) for i in range(n)])
        full = lax.dynamic_update_slice_in_dim(full, part, lax.rem(me - step + n, n) * width, axis)
    return full


def general(capacity, tokens, routes, route_gates, w_gate, w_up, w_down, cotangent):
    groups = lax.axis_size("expert")
    tok_rows, width = tokens.shape
    top_count = routes.shape[1]
    pair_expert = routes.reshape(-1)
    pair_token = jnp.arange(tok_rows * top_count, dtype=jnp.int32) // top_count
    onehot = (pair_expert[:, None] == jnp.arange(groups, dtype=jnp.int32)[None, :]).astype(F32)
    before = (pair_token.size, pair_token.size)
    before = lax.broadcasted_iota(jnp.int32, before, 0) > lax.broadcasted_iota(jnp.int32, before, 1)
    slot_rank = jnp.sum(dot(before.astype(F32), onehot) * onehot, axis=1).astype(jnp.int32)
    slot_place = pair_expert * capacity + slot_rank
    pair_gate = route_gates.reshape(-1)
    cot_pairs = cotangent[pair_token].astype(F32)
    row_grad = (pair_gate[:, None] * cot_pairs).astype(BF)

    def send(rows):
        box = jnp.zeros((groups * capacity, width), BF).at[slot_place].set(rows)
        return swap(box.reshape(groups, capacity, width)).reshape(groups * capacity, width)

    def swap(box):
        return lax.all_to_all(box, "expert", split_axis=0, concat_axis=0, tiled=True)

    def fetch(rows):
        back = swap(rows.astype(BF).reshape(groups, capacity, width))
        return back.reshape(groups * capacity, width)[slot_place].astype(F32)

    gate_full, up_full, down_full = gather(w_gate[0], 0), gather(w_up[0], 0), gather(w_down[0], 1)
    x = send(tokens[pair_token])
    gate_pre, up_pre = dot(x, gate_full), dot(x, up_full)
    sg = jax.nn.sigmoid(gate_pre)
    pair_out = fetch(dot((gate_pre * sg * up_pre).astype(BF), down_full))
    hid_grad = dot(send(row_grad), down_full, NT)
    pre_gate = (hid_grad * up_pre * sg * (1.0 + gate_pre * (1.0 - sg))).astype(BF)
    pre_up = (hid_grad * gate_pre * sg).astype(BF)
    pair_grad = fetch(dot(pre_gate, gate_full, NT) + dot(pre_up, up_full, NT))
    layer_out = jnp.sum((pair_gate[:, None] * pair_out).reshape(tok_rows, top_count, width), axis=1).astype(BF)
    gate_grad = jnp.sum(cot_pairs * pair_out, axis=1).reshape(tok_rows, top_count)
    token_grad = jnp.sum(pair_grad.reshape(tok_rows, top_count, width), axis=1).astype(BF)
    return (layer_out, token_grad, gate_grad)


def local(tokens, routes, route_gates, w_gate, w_up, w_down, cotangent):
    groups = lax.axis_size("expert")
    args = (tokens, routes, route_gates, w_gate, w_up, w_down, cotangent)
    capacity = 9 * tokens.shape[0] * routes.shape[1] // (8 * groups)
    main = capacity // 16 * 16
    rem = capacity - main
    if lax.axis_size("dp") == 4 and main and rem == 4 and tokens.shape[1] % 512 == 0 and groups * main <= 512:
        return fused(main, rem, *args)
    return general(capacity, *args)


def solution(mesh):
    rows = P(("dp", "expert"), None)
    in_specs = (rows, rows, rows, P("expert", "dp", None), P("expert", "dp", None), P("expert", None, "dp"), rows)
    return jax.shard_map(local, mesh=mesh, in_specs=in_specs, out_specs=(rows, rows, rows), check_vma=False)
```

time: 286 us -> 160 us (0.56); the launches traced: 282 us -> 160 us
  waiting for transfers between devices: 176 us -> 0 us
  Pallas kernels: 0 us -> 153 us
  starting transfers between devices: 24.8 us -> 0 us
  local copies, waits for them, and re-layouts: 29.9 us -> 6.51 us
  matrix products: 23 us -> 0 us
  other arithmetic: 14.1 us -> 0 us
  between operations: 13.9 us -> 0.65 us
    pallas_call x0 -> x1, Pallas kernels: none -> 153 us  [fused(): pl.pallas_call(functools.partial(moe_kernel, E, MAIN, REM), out_shape=(ja...]
    all_gather x3 -> x0, waiting for transfers between devices: 88.5 us -> none  [the longest x1 47.4 us: local(): lax.all_gather(w_down[0], 'dp', axis=1, tiled=True)]
    all_to_all x4 -> x0, waiting for transfers between devices: 85.9 us -> none  [the longest x1 30.4 us: local(): lax.all_to_all(outbox, 'expert', split_axis=0, concat_axis=0, tiled=True)]
    all_to_all x4 -> x0, starting transfers between devices: 24.7 us -> none  [the longest x1 6.86 us: local(): lax.all_to_all(gradbox, 'expert', split_axis=0, concat_axis=0, tiled=True)]
    dot_general x6 -> x0, matrix products: 23 us -> none  [the longest x1 5.1 us: expert_forward(): jnp.einsum('snf,fd->snd', hidden, down_full, preferred_element_type=jnp.f...]
    gather x4 -> x0, local copies, waits for them, and re-layouts: 10.6 us -> none  [the longest x2 6.62 us: local(): back_grad.reshape(groups * capacity, width)[slot_place].astype(jnp.float32)]
    reduce_sum x4 -> x0, other arithmetic: 10.4 us -> none  [the longest x1 5.34 us: local(): jnp.sum(pair_grad.reshape(tok_rows, top_count, width), axis=1)]
    scatter x1 -> x0, local copies, waits for them, and re-layouts: 6.87 us -> none  [local(): jnp.zeros((groups * capacity, width), jnp.bfloat16).at[slot_place]]
  transfers between devices with their start and end apart: 7 -> 0, of which waited for: 5 -> 0; matrix products, arithmetic and copies ran while one was open for 17% -> 0% of each run, Pallas kernels for 0% -> 0%
where the time goes in v1:
time: 160 us
  Pallas kernels  153 us (96%)
  local copies, waits for them, and re-layouts  6.51 us (4%)
    pallas_call x1, Pallas kernels, fused(): pl.pallas_call(functools.partial(moe_kernel, E, MAIN, REM), out_shape=(ja...  153 us
    unnamed x10, local copies, waits for them, and re-layouts  5.03 us

profile of v1, /device:TPU:25, one launch (start us, length us, event | category | flops | bytes accessed | tf_op | source)
XLA Modules:
  0.0 159.8 jit_solution(1047951192570244194)
XLA Ops:
  0.6 0.0 copy-start.1
  0.6 0.7 copy-done.1
  1.3 0.0 copy-start.2
  1.3 0.7 copy.10.routes_ref
  2.1 0.0 copy-done.2
  2.1 0.7 copy.11.gates_ref
  2.8 152.6 %shard_map.94 = (bf16[128,2560]{1,0:T(8,128)(2,1)}, bf16[128,2560]{1,0:T(8,128)(2,1)}, f32[128,2]{1,0:T(8,128)}) custom-call(bf16[128,2560]{1,0:T(8,128)(2,1)} %tok_ref.1, bf16[128,2560]{1,0:T(8,128)(2,1)} %cot_ref.1, s32[128,2]{1,0:T(8,128)} %copy.10.routes_ref, f32[128,2]{1,0:T(8,128)} %copy.11.gates_ref, s32[2,128]{1,0:T(2,128)} %bitcast.2, ...), custom_call_target="tpu_custom_call" | custom-call | tf_op jit(solution)/shard_map/pallas_call | solution.py:338
  155.4 1.5 copy.12
  156.9 0.0 copy-start
  156.9 2.0 %copy.15 = bf16[128,2560]{1,0:T(8,128)(2,1)} copy(bf16[128,2560]{1,0:T(8,128)(2,1)} %get-tuple-element.9) | data formatting | bytes 1310720
  158.9 0.0 copy-done
  159.0 0.8 copy.16
Async XLA Ops:
  0.6 0.7 copy-start.1
  1.3 0.7 copy-start.2
  156.9 2.0 %copy-start = (bf16[128,2560]{1,0:T(8,128)(2,1)S(1)}, bf16[128,2560]{1,0:T(8,128)(2,1)}, u32[]{:S(2)}) copy-start(bf16[128,2560]{1,0:T(8,128)(2,1)} %get-tuple-element.10) | copy-start | bytes 1966084

commit v2 on v1

--- a/solution.py
+++ b/solution.py
@@ -21,15 +21,15 @@
     E,
     MAIN,
     REM,
-    tok_ref, cot_ref, routes_ref, gates_ref, routes_t_ref, gates_t_ref,
+    tok_ref, cot_ref, routes_t_ref, gates_t_ref,
     wg_ref, wu_ref, wd_ref,
     lo_ref, tg_ref, gg_ref,
     wg, wu, wd,
     tok_out, grd_out, tok_in, grd_in,
     res_out, res_in, ig_out, ig_in,
     xs, gs, s_main, s_ext, p_main, p_ext,
-    gate_pre, up_pre, hid_grad, hidden, pre_gate, pre_up,
-    loc_sem, ws_sem, wr_sem,
+    gate_pre, up_pre, hid_grad, hidden, pre_gate, pre_up, ext_sum, ig_sum,
+    loc_sem, ws_sem, wr_sem, ds_sem, dr_sem,
     ts_sem, tr_sem, gs_sem, gr_sem,
     os_sem, or_sem, is_sem, ir_sem,
 ):
@@ -70,6 +70,18 @@
         b = (xp, yp)[j]
         return remote(src.at[0], buf.at[b], ws_sem.at[m, j], wr_sem.at[m, j], "dp", b)
 
+    CUT = (CB + 255) // 256 * 128
+    parts = ((0, CUT), (CUT, CB - CUT))
+
+    def down(j, h):
+        cols = pl.ds(*parts[h])
+        return remote(wd_ref.at[0, :, cols], wd.at[dp, :, cols], ds_sem.at[j, h], dr_sem.at[j, h], "dp", (xp, yp)[j])
+
+    def down_arrived(j, h):
+        cols = pl.ds(*parts[h])
+        b = (xp, yp)[j]
+        return remote(wd_ref.at[0, :, cols], wd.at[b, :, cols], ds_sem.at[j, h], dr_sem.at[j, h], "dp", b)
+
     def relay(m, j):
         buf = mats[m][1]
         half = buf.shape[1] // 2
@@ -100,26 +112,17 @@
     rank_t = dot(jnp.where(hit, 1.0, 0.0).astype(BF), jnp.where(before, 1.0, 0.0).astype(BF)).astype(jnp.int32)
     rank_t = jnp.where(hit, rank_t, -1)
     gate_t = jnp.where(hit0, g_t[0:1, :], 0.0) + jnp.where(hit1, g_t[1:2, :], 0.0)
-    gsel, gsel_x = [], []
     row_m = lax.broadcasted_iota(jnp.int32, (MAIN, T), 0)
     row_x = lax.broadcasted_iota(jnp.int32, (16, T), 0)
     for e in range(E):
         rank_e = rank_t[e : e + 1, :]
-        gate_e = gate_t[e : e + 1, :]
-        sel = row_m == rank_e
-        s_main[pl.ds(e * MAIN, MAIN), :] = jnp.where(sel, 1.0, 0.0).astype(BF)
-        gsel.append(jnp.sum(jnp.where(sel, gate_e, 0.0), axis=1, keepdims=True))
-        total = jnp.zeros((16, 1), F32)
+        s_main[pl.ds(e * MAIN, MAIN), :] = jnp.where(row_m == rank_e, 1.0, 0.0).astype(BF)
         for q in range(FOLD):
             sel = jnp.logical_and(
                 row_x - q * REM + MAIN == rank_e,
                 jnp.logical_and(rank_e >= MAIN, jnp.logical_and(row_x >= q * REM, row_x < q * REM + REM)),
             )
             s_ext[q, pl.ds(e * 16, 16), :] = jnp.where(sel, 1.0, 0.0).astype(BF)
-            total = total + jnp.sum(jnp.where(sel, gate_e, 0.0), axis=1, keepdims=True)
-        gsel_x.append(total)
-    gsel = jnp.concatenate(gsel, axis=0)
-    gsel_x = jnp.concatenate(gsel_x, axis=0)
 
     def pack(src_ref, box, scale, scale_x):
         ext = jnp.zeros((EXT, CB), F32)
@@ -146,24 +149,33 @@
     for o in range(1, E):
         exchange(tok_out, tok_in, ts_sem, tr_sem, o).start()
     tok_in[pl.ds(me, 1)] = tok_out[pl.ds(me, 1)]
-    pack(cot_ref, grd_out, gsel, gsel_x)
+    gsel, gsel_x = [], []
+    for e in range(E):
+        gate_e = gate_t[e : e + 1, :]
+        sel = s_main[pl.ds(e * MAIN, MAIN), :].astype(F32)
+        gsel.append(jnp.sum(sel * gate_e, axis=1, keepdims=True))
+        sel = sum(s_ext[q, pl.ds(e * 16, 16), :].astype(F32) for q in range(FOLD))
+        gsel_x.append(jnp.sum(sel * gate_e, axis=1, keepdims=True))
+    pack(cot_ref, grd_out, jnp.concatenate(gsel, axis=0), jnp.concatenate(gsel_x, axis=0))
     for o in range(1, E):
         exchange(grd_out, grd_in, gs_sem, gr_sem, o).start()
     grd_in[pl.ds(me, 1)] = grd_out[pl.ds(me, 1)]
 
-    lane_t = lax.broadcasted_iota(jnp.int32, (T, 128), 1)
-    e_of = [routes_ref[:, k : k + 1] for k in range(2)]
-    named = jnp.logical_or(e_of[0] == lane_t, e_of[1] == lane_t)
-    after = lax.broadcasted_iota(jnp.int32, (T, T), 0) > lax.broadcasted_iota(jnp.int32, (T, T), 1)
-    rank = dot(jnp.where(after, 1.0, 0.0).astype(BF), jnp.where(named, 1.0, 0.0).astype(BF))
+    ranks = rank_t.astype(F32)
+    turned = [r_t[k : k + 1, :].astype(F32) for k in range(2)]
+    turned += [jnp.sum(jnp.where(h, ranks, 0.0), axis=0, keepdims=True) for h in (hit0, hit1)]
+    turned += [g_t[0:1, :], g_t[1:2, :], jnp.zeros((2, T), F32)]
+    turned = jnp.concatenate(turned, axis=0).T
+    gates = [turned[:, 4 + k : 5 + k] for k in range(2)]
     lane_m = lax.broadcasted_iota(jnp.int32, (T, ROWS), 1)
     lane_x = lax.broadcasted_iota(jnp.int32, (T, EXT), 1)
     for k in range(2):
-        rk = jnp.sum(jnp.where(lane_t == e_of[k], rank, 0.0), axis=1, keepdims=True).astype(jnp.int32)
-        place = jnp.where(rk < MAIN, e_of[k] * MAIN + rk, -1)
+        e_k = turned[:, k : k + 1].astype(jnp.int32)
+        rk = turned[:, 2 + k : 3 + k].astype(jnp.int32)
+        place = jnp.where(rk < MAIN, e_k * MAIN + rk, -1)
         p_main[k] = jnp.where(lane_m == place, 1.0, 0.0).astype(BF)
         for q in range(FOLD):
-            place = jnp.where(rk >= MAIN, e_of[k] * 16 + q * REM + rk - MAIN, -1)
+            place = jnp.where(rk >= MAIN, e_k * 16 + q * REM + rk - MAIN, -1)
             p_ext[k, q] = jnp.where(lane_x == place, 1.0, 0.0).astype(BF)
 
     for m in range(2):
@@ -190,30 +202,32 @@
             dst[b, pl.ds(0, ROWS), :] = box[:, pl.ds(b * MAIN, MAIN), :].reshape(ROWS, CB)
             dst[b, pl.ds(ROWS, UNF), :] = dot(unfold(b), ext).astype(BF)
 
+    for j in range(2):
+        relay_arrived(0, j).wait_recv()
+    for h in range(2):
+        for j in range(2):
+            down(j, h).start()
     for o in range(1, E):
         arrived(tok_out, tok_in, ts_sem, tr_sem, o).wait_recv()
     unpack(tok_in, xs)
     locs[0].wait()
     locs[1].wait()
-    for j in range(2):
-        relay_arrived(0, j).wait_recv()
-    own(2, 0).start()
-    own(2, 1).start()
-
-    def add_gate(b, c):
+
+    def add_gate(b):
         gate_pre[...] += dot(xs[b], wg[b])
-        return c
-
-    def add_up(b, c):
+
+    def add_up(b):
         up_pre[...] += dot(xs[b], wu[b])
-        return c
-
-    gate_pre[...] = jnp.zeros_like(gate_pre)
-    up_pre[...] = jnp.zeros_like(up_pre)
-    lax.fori_loop(0, NB, add_gate, 0)
+
+    gate_pre[...] = dot(xs[dp], wg[dp])
+    up_pre[...] = dot(xs[dp], wu[dp])
+    for b in (xp, yp):
+        add_gate(b)
+        add_up(b)
+    add_gate(dg)
     for j in range(2):
         relay_arrived(1, j).wait_recv()
-    lax.fori_loop(0, NB, add_up, 0)
+    add_up(dg)
     gp = gate_pre[...]
     hidden[...] = (gp * jax.nn.sigmoid(gp) * up_pre[...]).astype(BF)
 
@@ -221,26 +235,40 @@
         part = pl.ds(start, size)
         return remote(src.at[to, part], dst.at[at, part], s.at[i, o], r.at[i, o], "expert", to)
 
-    ext_sum = [jnp.zeros((EXT, CB), F32)]
-
-    def result(i, b):
-        out = dot(hidden[...], wd[b]).astype(BF)
+    steps = [(dp, 0, CB)] + [(b, *part) for part in parts for b in (xp, yp)] + [(dg, 0, CB)]
+    LAST = len(steps)
+
+    def back_out(i, o, to, at):
+        b, first, width = steps[i]
+        part = (pl.ds(pl.multiple_of(b * MAIN, MAIN), MAIN), pl.ds(first, width))
+        return remote(
+            res_out.at[(to, *part)], res_in.at[(at, *part)], os_sem.at[i, o], or_sem.at[i, o], "expert", to
+        )
+
+    ext_sum[...] = jnp.zeros_like(ext_sum)
+
+    def result(i):
+        b, first, width = steps[i]
+        cols = slice(first, first + width)
+        out = dot(hidden[...], wd[b, :, cols]).astype(BF)
         start = pl.multiple_of(b * MAIN, MAIN)
-        res_out[:, pl.ds(start, MAIN), :] = out[:ROWS].reshape(E, MAIN, CB)
+        res_out[:, pl.ds(start, MAIN), cols] = out[:ROWS].reshape(E, MAIN, width)
         for o in range(1, E):
-            back(res_out, res_in, os_sem, or_sem, i, o, start, MAIN, lax.rem(me + o, E), me).start()
-        ext_sum[0] = ext_sum[0] + dot(fold(b), out[ROWS:])
+            back_out(i, o, lax.rem(me + o, E), me).start()
+        ext_sum[:, cols] += dot(fold(b), out[ROWS:])
 
     locs[2].wait()
-    result(0, dp)
+    result(0)
     for o in range(1, E):
         arrived(grd_out, grd_in, gs_sem, gr_sem, o).wait_recv()
     unpack(grd_in, gs)
-    for j in range(2):
-        own_arrived(2, j).wait_recv()
-        relay(2, j).start()
-    result(1, xp)
-    result(2, yp)
+    for h in range(2):
+        for j in range(2):
+            down_arrived(j, h).wait_recv()
+            if h == 1:
+                relay(2, j).start()
+        result(1 + 2 * h)
+        result(2 + 2 * h)
 
     def add_grad(b):
         hid_grad[...] += dot(gs[b], wd[b], NT)
@@ -250,10 +278,10 @@
         add_grad(b)
     for j in range(2):
         relay_arrived(2, j).wait_recv()
-    result(3, dg)
-    res_out[:, pl.ds(XROW, 16), :] = ext_sum[0].astype(BF).reshape(E, 16, CB)
-    for o in range(1, E):
-        back(res_out, res_in, os_sem, or_sem, 4, o, XROW, 16, lax.rem(me + o, E), me).start()
+    result(LAST - 1)
+    res_out[:, pl.ds(XROW, 16), :] = ext_sum[...].astype(BF).reshape(E, 16, CB)
+    for o in range(1, E):
+        back(res_out, res_in, os_sem, or_sem, LAST, o, XROW, 16, lax.rem(me + o, E), me).start()
     res_in[pl.ds(me, 1)] = res_out[pl.ds(me, 1)]
     add_grad(dg)
 
@@ -276,13 +304,13 @@
             back(ig_out, ig_in, is_sem, ir_sem, b, o, b * MAIN, size, lax.rem(me + o, E), me).start()
     ig_in[pl.ds(me, 1)] = ig_out[pl.ds(me, 1)]
 
-    for i, b in enumerate((dp, xp, yp, dg)):
+    for i in range(LAST):
         for o in range(1, E):
             frm = lax.rem(me + E - o, E)
-            back(res_out, res_in, os_sem, or_sem, i, o, pl.multiple_of(b * MAIN, MAIN), MAIN, frm, frm).wait_recv()
+            back_out(i, o, frm, frm).wait_recv()
     for o in range(1, E):
         frm = lax.rem(me + E - o, E)
-        back(res_out, res_in, os_sem, or_sem, 4, o, XROW, 16, frm, frm).wait_recv()
+        back(res_out, res_in, os_sem, or_sem, LAST, o, XROW, 16, frm, frm).wait_recv()
 
     def pairs(box, b, ext):
         rows = box[:, pl.ds(b * MAIN, MAIN), :].reshape(ROWS, CB)
@@ -294,31 +322,40 @@
         cols = slice(b * CB, (b + 1) * CB)
         two = pairs(res_in, b, ext)
         cot = cot_ref[:, cols].astype(F32)
-        lo_ref[:, cols] = (gates_ref[:, 0:1] * two[0] + gates_ref[:, 1:2] * two[1]).astype(BF)
+        lo_ref[:, cols] = (gates[0] * two[0] + gates[1] * two[1]).astype(BF)
         dots = [dots[k] + jnp.sum(cot * two[k], axis=1, keepdims=True) for k in range(2)]
-    gg_ref[...] = jnp.concatenate(dots, axis=1)
-
+    lane = lax.broadcasted_iota(jnp.int32, (T, 8), 1)
+    gg_ref[...] = jnp.where(lane == 0, dots[0], jnp.where(lane == 1, dots[1], 0.0)).T[0:2, :]
+
+    both = p_main[0] + p_main[1]
     for b in range(NB):
         size = MAIN + 16 if b == NB - 1 else MAIN
         for o in range(1, E):
             frm = lax.rem(me + E - o, E)
             back(ig_out, ig_in, is_sem, ir_sem, b, o, b * MAIN, size, frm, frm).wait_recv()
-    ext = ig_in[:, pl.ds(XROW, 16), :].reshape(EXT, CB)
-    for b in range(NB):
-        two = pairs(ig_in, b, ext)
-        tg_ref[:, b * CB : (b + 1) * CB] = (two[0] + two[1]).astype(BF)
-
-    for m in range(3):
-        for j in range(2):
+        rows = ig_in[:, pl.ds(b * MAIN, MAIN), :].reshape(ROWS, CB)
+        if b < NB - 1:
+            ig_sum[b] = dot(both, rows)
+        else:
+            ext = ig_in[:, pl.ds(XROW, 16), :].reshape(EXT, CB)
+            tg_ref[:, b * CB :] = (dot(both, rows) + dot(p_ext[0, b] + p_ext[1, b], ext)).astype(BF)
+    for b in range(NB - 1):
+        total = ig_sum[b] + dot(p_ext[0, b] + p_ext[1, b], ext)
+        tg_ref[:, b * CB : (b + 1) * CB] = total.astype(BF)
+
+    for j in range(2):
+        for m in range(3):
+            relay(m, j).wait_send()
+        for m in range(2):
             own(m, j).wait_send()
-            relay(m, j).wait_send()
+            down(j, m).wait_send()
     for o in range(1, E):
         exchange(tok_out, tok_in, ts_sem, tr_sem, o).wait_send()
         exchange(grd_out, grd_in, gs_sem, gr_sem, o).wait_send()
         to = lax.rem(me + o, E)
-        for i, b in enumerate((dp, xp, yp, dg)):
-            back(res_out, res_in, os_sem, or_sem, i, o, pl.multiple_of(b * MAIN, MAIN), MAIN, to, me).wait_send()
-        back(res_out, res_in, os_sem, or_sem, 4, o, XROW, 16, to, me).wait_send()
+        for i in range(LAST):
+            back_out(i, o, to, me).wait_send()
+        back(res_out, res_in, os_sem, or_sem, LAST, o, XROW, 16, to, me).wait_send()
         for b in range(NB):
             size = MAIN + 16 if b == NB - 1 else MAIN
             back(ig_out, ig_in, is_sem, ir_sem, b, o, b * MAIN, size, to, me).wait_send()
@@ -335,14 +372,14 @@
     vm = pl.BlockSpec(memory_space=pltpu.VMEM)
     hb = pl.BlockSpec(memory_space=pl.ANY)
     dma = pltpu.SemaphoreType.DMA
-    return pl.pallas_call(
+    layer_out, token_grad, gate_grad = pl.pallas_call(
         functools.partial(moe_kernel, E, MAIN, REM),
         out_shape=(
             jax.ShapeDtypeStruct((T, D), BF),
             jax.ShapeDtypeStruct((T, D), BF),
-            jax.ShapeDtypeStruct((T, 2), F32),
+            jax.ShapeDtypeStruct((2, T), F32),
         ),
-        in_specs=[vm] * 6 + [hb] * 3,
+        in_specs=[vm] * 4 + [hb] * 3,
         out_specs=(vm, vm, vm),
         scratch_shapes=[
             pltpu.VMEM((4, CB, FF), BF), pltpu.VMEM((4, CB, FF), BF), pltpu.VMEM((4, FF, CB), BF),
@@ -352,15 +389,16 @@
             pltpu.VMEM((E * MAIN, T), BF), pltpu.VMEM((16 // REM, E * 16, T), BF),
             pltpu.VMEM((2, T, E * MAIN), BF), pltpu.VMEM((2, 16 // REM, T, E * 16), BF),
             pltpu.VMEM((R, FF), F32), pltpu.VMEM((R, FF), F32), pltpu.VMEM((R, FF), F32),
-            pltpu.VMEM((R, FF), BF), pltpu.VMEM((R, FF), BF), pltpu.VMEM((R, FF), BF),
-            dma((3,)), dma((3, 4)), dma((3, 4)),
+            pltpu.VMEM((R, FF), BF), pltpu.VMEM((R, FF), BF), pltpu.VMEM((R, FF), BF), pltpu.VMEM((E * 16, CB), F32), pltpu.VMEM((3, T, CB), F32),
+            dma((3,)), dma((3, 4)), dma((3, 4)), dma((2, 2)), dma((2, 2)),
             dma((E,)), dma((E,)), dma((E,)), dma((E,)),
-            dma((5, E)), dma((5, E)), dma((4, E)), dma((4, E)),
+            dma((7, E)), dma((7, E)), dma((4, E)), dma((4, E)),
         ],
         compiler_params=pltpu.CompilerParams(
             collective_id=0, has_side_effects=True, vmem_limit_bytes=56 * 1024 * 1024
         ),
-    )(tokens, cotangent, routes, route_gates, routes.T, route_gates.T, w_gate, w_up, w_down)
+    )(tokens, cotangent, routes.T, route_gates.T, w_gate, w_up, w_down)
+    return layer_out, token_grad, gate_grad.T
 
 
 def gather(x, axis):

time: 160 us -> 155 us (0.969)
  local copies, waits for them, and re-layouts: 6.51 us -> 3.44 us
  Pallas kernels: 153 us -> 150 us
    pallas_call x1, Pallas kernels: 153 us -> 150 us  [fused(): pl.pallas_call(functools.partial(moe_kernel, E, MAIN, REM), out_shape=(ja...]
    unnamed x10 -> x7, local copies, waits for them, and re-layouts: 5.03 us -> 3.44 us
where the time goes in v2:
time: 155 us
  Pallas kernels  150 us (97%)
  local copies, waits for them, and re-layouts  3.44 us (2%)
    pallas_call x1, Pallas kernels, fused(): pl.pallas_call(functools.partial(moe_kernel, E, MAIN, REM), out_shape=(ja...  150 us
    unnamed x7, local copies, waits for them, and re-layouts  3.44 us

profile of v2, /device:TPU:25, one launch (start us, length us, event | category | flops | bytes accessed | tf_op | source)
XLA Modules:
  0.0 154.5 jit_solution(3781831873919737798)
XLA Ops:
  0.6 150.4 %shard_map.94 = (bf16[128,2560]{1,0:T(8,128)(2,1)}, bf16[128,2560]{1,0:T(8,128)(2,1)}, f32[2,128]{1,0:T(2,128)}) custom-call(bf16[128,2560]{1,0:T(8,128)(2,1)} %tok_ref.1, bf16[128,2560]{1,0:T(8,128)(2,1)} %cot_ref.1, s32[2,128]{1,0:T(2,128)} %bitcast.4, f32[2,128]{1,0:T(2,128)} %bitcast.5, bf16[1,640,768]{2,1,0:T(8,128)(2,1)} %wg_ref.1, ...), custom_call_target="tpu_custom_call" | custom-call | tf_op jit(solution)/shard_map/pallas_call | solution.py:375
  151.1 0.0 copy-start
  151.1 2.0 %copy.13 = bf16[128,2560]{1,0:T(8,128)(2,1)} copy(bf16[128,2560]{1,0:T(8,128)(2,1)} %get-tuple-element.12) | data formatting | bytes 1310720
  153.1 0.0 copy-done
  153.1 0.0 copy-start.1
  153.1 0.8 copy.14
  154.0 0.0 copy-done.1
  154.0 0.6 copy.15
Async XLA Ops:
  151.1 2.0 %copy-start = (bf16[128,2560]{1,0:T(8,128)(2,1)S(1)}, bf16[128,2560]{1,0:T(8,128)(2,1)}, u32[]{:S(2)}) copy-start(bf16[128,2560]{1,0:T(8,128)(2,1)} %get-tuple-element.13) | copy-start | bytes 1966084
  153.1 0.8 copy-start.1

commit v3 on v2

--- a/solution.py
+++ b/solution.py
@@ -157,8 +157,6 @@
         sel = sum(s_ext[q, pl.ds(e * 16, 16), :].astype(F32) for q in range(FOLD))
         gsel_x.append(jnp.sum(sel * gate_e, axis=1, keepdims=True))
     pack(cot_ref, grd_out, jnp.concatenate(gsel, axis=0), jnp.concatenate(gsel_x, axis=0))
-    for o in range(1, E):
-        exchange(grd_out, grd_in, gs_sem, gr_sem, o).start()
     grd_in[pl.ds(me, 1)] = grd_out[pl.ds(me, 1)]
 
     ranks = rank_t.astype(F32)
@@ -178,11 +176,6 @@
             place = jnp.where(rk >= MAIN, e_k * 16 + q * REM + rk - MAIN, -1)
             p_ext[k, q] = jnp.where(lane_x == place, 1.0, 0.0).astype(BF)
 
-    for m in range(2):
-        for j in range(2):
-            own_arrived(m, j).wait_recv()
-            relay(m, j).start()
-
     u_row = lax.broadcasted_iota(jnp.int32, (UNF, EXT), 0)
     u_col = lax.broadcasted_iota(jnp.int32, (UNF, EXT), 1)
     f_row = lax.broadcasted_iota(jnp.int32, (EXT, UNF), 0)
@@ -202,28 +195,36 @@
             dst[b, pl.ds(0, ROWS), :] = box[:, pl.ds(b * MAIN, MAIN), :].reshape(ROWS, CB)
             dst[b, pl.ds(ROWS, UNF), :] = dot(unfold(b), ext).astype(BF)
 
+    for o in range(1, E):
+        exchange(tok_out, tok_in, ts_sem, tr_sem, o).wait_send()
+    for o in range(1, E):
+        exchange(grd_out, grd_in, gs_sem, gr_sem, o).start()
+    for o in range(1, E):
+        arrived(tok_out, tok_in, ts_sem, tr_sem, o).wait_recv()
+    unpack(tok_in, xs)
+    locs[0].wait()
+    locs[1].wait()
+
+    def add_gate(b):
+        gate_pre[...] += dot(xs[b], wg[b])
+
+    def add_up(b):
+        up_pre[...] += dot(xs[b], wu[b])
+
+    gate_pre[...] = dot(xs[dp], wg[dp])
+    up_pre[...] = dot(xs[dp], wu[dp])
+    for m in range(2):
+        for j in range(2):
+            own_arrived(m, j).wait_recv()
+            relay(m, j).start()
+    for b in (xp, yp):
+        add_gate(b)
+        add_up(b)
     for j in range(2):
         relay_arrived(0, j).wait_recv()
     for h in range(2):
         for j in range(2):
             down(j, h).start()
-    for o in range(1, E):
-        arrived(tok_out, tok_in, ts_sem, tr_sem, o).wait_recv()
-    unpack(tok_in, xs)
-    locs[0].wait()
-    locs[1].wait()
-
-    def add_gate(b):
-        gate_pre[...] += dot(xs[b], wg[b])
-
-    def add_up(b):
-        up_pre[...] += dot(xs[b], wu[b])
-
-    gate_pre[...] = dot(xs[dp], wg[dp])
-    up_pre[...] = dot(xs[dp], wu[dp])
-    for b in (xp, yp):
-        add_gate(b)
-        add_up(b)
     add_gate(dg)
     for j in range(2):
         relay_arrived(1, j).wait_recv()
@@ -301,6 +302,14 @@
             ig_out[:, pl.ds(XROW, 16), :] = ext.astype(BF).reshape(E, 16, CB)
             size = MAIN + 16
         for o in range(1, E):
+            to = lax.rem(me + o, E)
+            for i in ((0, 1, 2), (3, 4), (5,), ())[b]:
+                back_out(i, o, to, me).wait_send()
+            if b == 2:
+                back(res_out, res_in, os_sem, or_sem, LAST, o, XROW, 16, to, me).wait_send()
+            if b == 3:
+                back(ig_out, ig_in, is_sem, ir_sem, 0, o, 0, MAIN, to, me).wait_send()
+        for o in range(1, E):
             back(ig_out, ig_in, is_sem, ir_sem, b, o, b * MAIN, size, lax.rem(me + o, E), me).start()
     ig_in[pl.ds(me, 1)] = ig_out[pl.ds(me, 1)]
 
@@ -350,13 +359,9 @@
             own(m, j).wait_send()
             down(j, m).wait_send()
     for o in range(1, E):
-        exchange(tok_out, tok_in, ts_sem, tr_sem, o).wait_send()
         exchange(grd_out, grd_in, gs_sem, gr_sem, o).wait_send()
         to = lax.rem(me + o, E)
-        for i in range(LAST):
-            back_out(i, o, to, me).wait_send()
-        back(res_out, res_in, os_sem, or_sem, LAST, o, XROW, 16, to, me).wait_send()
-        for b in range(NB):
+        for b in range(1, NB):
             size = MAIN + 16 if b == NB - 1 else MAIN
             back(ig_out, ig_in, is_sem, ir_sem, b, o, b * MAIN, size, to, me).wait_send()
 

time: 155 us -> 157 us (1.013)
  Pallas kernels: 150 us -> 152 us
    pallas_call x1, Pallas kernels: 150 us -> 152 us  [fused(): pl.pallas_call(functools.partial(moe_kernel, E, MAIN, REM), out_shape=(ja...]
where the time goes in v3:
time: 157 us; the launch traced here: 156 us
  Pallas kernels  152 us (97%)
  local copies, waits for them, and re-layouts  3.44 us (2%)
    pallas_call x1, Pallas kernels, fused(): pl.pallas_call(functools.partial(moe_kernel, E, MAIN, REM), out_shape=(ja...  152 us
    unnamed x7, local copies, waits for them, and re-layouts  3.44 us

profile of v3, /device:TPU:25, one launch (start us, length us, event | category | flops | bytes accessed | tf_op | source)
XLA Modules:
  0.0 156.3 jit_solution(11711141774663432582)
XLA Ops:
  0.6 152.2 %shard_map.94 = (bf16[128,2560]{1,0:T(8,128)(2,1)}, bf16[128,2560]{1,0:T(8,128)(2,1)}, f32[2,128]{1,0:T(2,128)}) custom-call(bf16[128,2560]{1,0:T(8,128)(2,1)} %tok_ref.1, bf16[128,2560]{1,0:T(8,128)(2,1)} %cot_ref.1, s32[2,128]{1,0:T(2,128)} %bitcast.4, f32[2,128]{1,0:T(2,128)} %bitcast.5, bf16[1,640,768]{2,1,0:T(8,128)(2,1)} %wg_ref.1, ...), custom_call_target="tpu_custom_call" | custom-call | tf_op jit(solution)/shard_map/pallas_call | solution.py:380
  152.9 0.0 copy-start
  152.9 2.0 %copy.13 = bf16[128,2560]{1,0:T(8,128)(2,1)} copy(bf16[128,2560]{1,0:T(8,128)(2,1)} %get-tuple-element.12) | data formatting | bytes 1310720
  154.9 0.0 copy-done
  154.9 0.0 copy-start.1
  154.9 0.8 copy.14
  155.7 0.0 copy-done.1
  155.7 0.6 copy.15
Async XLA Ops:
  152.9 2.0 %copy-start = (bf16[128,2560]{1,0:T(8,128)(2,1)S(1)}, bf16[128,2560]{1,0:T(8,128)(2,1)}, u32[]{:S(2)}) copy-start(bf16[128,2560]{1,0:T(8,128)(2,1)} %get-tuple-element.13) | copy-start | bytes 1966084
  154.9 0.8 copy-start.1

commit v4 on v2

--- a/solution.py
+++ b/solution.py
@@ -182,6 +182,9 @@
         for j in range(2):
             own_arrived(m, j).wait_recv()
             relay(m, j).start()
+    for h in range(2):
+        for j in range(2):
+            down(j, h).start()
 
     u_row = lax.broadcasted_iota(jnp.int32, (UNF, EXT), 0)
     u_col = lax.broadcasted_iota(jnp.int32, (UNF, EXT), 1)
@@ -202,11 +205,6 @@
             dst[b, pl.ds(0, ROWS), :] = box[:, pl.ds(b * MAIN, MAIN), :].reshape(ROWS, CB)
             dst[b, pl.ds(ROWS, UNF), :] = dot(unfold(b), ext).astype(BF)
 
-    for j in range(2):
-        relay_arrived(0, j).wait_recv()
-    for h in range(2):
-        for j in range(2):
-            down(j, h).start()
     for o in range(1, E):
         arrived(tok_out, tok_in, ts_sem, tr_sem, o).wait_recv()
     unpack(tok_in, xs)
@@ -224,6 +222,8 @@
     for b in (xp, yp):
         add_gate(b)
         add_up(b)
+    for j in range(2):
+        relay_arrived(0, j).wait_recv()
     add_gate(dg)
     for j in range(2):
         relay_arrived(1, j).wait_recv()

time: 155 us -> 155 us (level)
  no operation moved by 1% of the time
where the time goes in v4:
time: 155 us
  Pallas kernels  150 us (97%)
  local copies, waits for them, and re-layouts  3.44 us (2%)
    pallas_call x1, Pallas kernels, fused(): pl.pallas_call(functools.partial(moe_kernel, E, MAIN, REM), out_shape=(ja...  150 us
    unnamed x7, local copies, waits for them, and re-layouts  3.44 us

profile of v4, /device:TPU:25, one launch (start us, length us, event | category | flops | bytes accessed | tf_op | source)
XLA Modules:
  0.0 154.5 jit_solution(10617080678430853152)
XLA Ops:
  0.6 150.4 %shard_map.94 = (bf16[128,2560]{1,0:T(8,128)(2,1)}, bf16[128,2560]{1,0:T(8,128)(2,1)}, f32[2,128]{1,0:T(2,128)}) custom-call(bf16[128,2560]{1,0:T(8,128)(2,1)} %tok_ref.1, bf16[128,2560]{1,0:T(8,128)(2,1)} %cot_ref.1, s32[2,128]{1,0:T(2,128)} %bitcast.4, f32[2,128]{1,0:T(2,128)} %bitcast.5, bf16[1,640,768]{2,1,0:T(8,128)(2,1)} %wg_ref.1, ...), custom_call_target="tpu_custom_call" | custom-call | tf_op jit(solution)/shard_map/pallas_call | solution.py:375
  151.1 0.0 copy-start
  151.1 2.0 %copy.13 = bf16[128,2560]{1,0:T(8,128)(2,1)} copy(bf16[128,2560]{1,0:T(8,128)(2,1)} %get-tuple-element.12) | data formatting | bytes 1310720
  153.1 0.0 copy-done
  153.1 0.0 copy-start.1
  153.1 0.8 copy.14
  154.0 0.0 copy-done.1
  154.0 0.6 copy.15
Async XLA Ops:
  151.1 2.0 %copy-start = (bf16[128,2560]{1,0:T(8,128)(2,1)S(1)}, bf16[128,2560]{1,0:T(8,128)(2,1)}, u32[]{:S(2)}) copy-start(bf16[128,2560]{1,0:T(8,128)(2,1)} %get-tuple-element.13) | copy-start | bytes 1966084
  153.1 0.8 copy-start.1
